TPU v7x, 512 devices: a whole 4x4x16 slice. The times are simulated.
512 devices in a mesh: term: 32 (over y, x, core), sector: 16 (over z).
Axes of the slice: x: 4, y: 4, z: 16, core: 2. Of those that a mesh axis runs over, the one named last changes fastest.
Arguments:
- wavefunction: bfloat16 [96, 256, 256], P('sector')
- left_operator_blocks: bfloat16 [384, 256, 256], P('term'), may hold values from -0.01953125 to 0.01953125
- right_operator_blocks: bfloat16 [384, 256, 256], P('term'), may hold values from -0.375 to 0.375
- fetch_index: int32 [32, 16, 16], P('term', 'sector'), may hold values from 0 to 5, as said below
- owner_link: int32 [384, 96], P('term', 'sector'), may hold values from 0 to 15, as said below
- lower_roots: bfloat16 [4, 96, 256, 256], P(None, 'sector', 'term')
- level_shift: float32 [4], replicated, may hold values from 0.5 to 2
Outputs:
- sigma: float32 [96, 256, 256], P('sector', 'term')
- correlations: float32 [4], replicated
Inputs may be any that keep to these rules, and one draw needn't show every extreme that they name: `fetch_index`: entry p of every list is a position within the 6 sectors of sector index p. `owner_link`: within the 12 x 6 entries that one device holds, every sector index occurs at least once.
All inputs are finite; a program needn't handle non-finite values.
Results may differ from a plain program's by a relative error of at most 0.0059.
Values may be sent and summed in bfloat16 or wider, within the bound.
A program may use at most 64 MiB of HBM per device.

v0:
```python
import jax
import jax.numpy as jnp
from jax import lax
from jax.sharding import PartitionSpec as P


def per_device(
    wavefunction,
    left_operator_blocks,
    right_operator_blocks,
    fetch_index,
    owner_link,
    lower_roots,
    level_shift,
):
    sec_dev = wavefunction.shape[0]
    block_width = wavefunction.shape[1]
    group_count = fetch_index.shape[2]
    own_requests = fetch_index.reshape(group_count, 1)
    store = lax.all_gather(wavefunction, "sector", axis=0, tiled=True)
    lookup = owner_link * sec_dev + own_requests[:, 0][owner_link]

    def one_sector(column):
        input_sectors = store[column]
        partial_contraction = jnp.einsum(
            "lhm,lmp->lhp", left_operator_blocks, input_sectors, preferred_element_type=jnp.float32
        ).astype(jnp.bfloat16)
        return jnp.einsum(
            "yxz,ysz->xs",
            partial_contraction,
            right_operator_blocks,
            preferred_element_type=jnp.float32,
        )

    partial_value = lax.map(one_sector, jnp.transpose(lookup))
    reduced = lax.psum_scatter(partial_value, "term", scatter_dimension=1, tiled=True)
    row_count = reduced.shape[1]
    row_start = lax.axis_index("term") * row_count
    psi_rows = lax.dynamic_slice_in_dim(wavefunction, row_start, row_count, 1)
    local_correlation = jnp.einsum(
        "ksab,sab->k", lower_roots, psi_rows, preferred_element_type=jnp.float32
    )
    total_cells = lax.axis_size("sector") * sec_dev * block_width * block_width
    correlations = lax.psum(local_correlation, ("term", "sector")) / total_cells
    sigma = reduced + jnp.einsum(
        "k,ksab->sab", level_shift * correlations, lower_roots.astype(jnp.float32)
    )
    return (sigma, correlations)


def solution(mesh):
    return jax.shard_map(
        per_device,
        mesh=mesh,
        in_specs=(
            P("sector", None, None),
            P("term", None, None),
            P("term", None, None),
            P("term", "sector", None),
            P("term", "sector"),
            P(None, "sector", "term", None),
            P(),
        ),
        out_specs=(P("sector", "term", None), P()),
        check_vma=False,
    )
```

profile of v0, /device:TPU:1, one launch (start us, length us, event | category | flops | bytes accessed | tf_op | source)
XLA Modules:
  0.0 328.3 jit_solution(2077307641894323809)
XLA Ops:
  7.2 0.7 all-gather.2.cloned.1.call-update
  8.0 0.8 copy.17
  8.8 0.7 compare_select_fusion.1
  9.4 0.1 copy.18
  9.7 1.2 gather_fusion.1
  11.1 152.4 %all-gather.2.cloned.1.call-done = bf16[96,256,256]{2,1,0:T(8,128)(2,1)} async-done(((bf16[6,256,256]{2,1,0:T(8,128)(2,1)}), bf16[96,256,256]{2,1,0:T(8,128)(2,1)}) %all-gather.2.cloned.1.call-update) | async-done | bytes 12582928 | tf_op jit(solution)/shard_map/all_gather | solution.py:20
  163.5 52.1 %while.10 = (s32[]{:T(128)}, f32[6,256,256]{2,1,0:T(8,128)}, s32[6,12]{1,0:T(8,128)S(1)}, bf16[96,256,256]{2,1,0:T(8,128)(2,1)}, bf16[12,256,256]{2,1,0:T(8,128)...) while((s32[]{:T(128)}, f32[6,256,256]{2,1,0:T(8,128)}, s32[6,12]{1,0:T(8,128)S(1)}, ...), condition=%wide.region_1.2_spmd, body=%wide.region_0.1_spmd.sunk | while | flops 806093888 | bytes 8130845 | solution.py:35
  163.5 5.2 %gather_fusion = bf16[12,256,256]{2,1,0:T(8,128)(2,1)S(1)} fusion(bf16[96,256,256]{2,1,0:T(8,128)(2,1)} %get-tuple-element.119, s32[1024]{0:T(1024)S(1)} %pad_clamp_fusion.3), kind=kCustom, calls=%fused_computation.clone.1 | custom fusion | bytes 3145776 | tf_op jit(solution)/shard_map/while/body/eval_jaxpr/gather | solution.py:24
  168.8 3.4 %fusion.27 = f32[6,256,256]{2,1,0:T(8,128)} fusion(f32[6,256,256]{2,1,0:T(8,128)} %get-tuple-element.110, s32[]{:T(128)S(6)} %copy.38, bf16[12,256,256]{2,1,0:T(8,128)(2,1)} %get-tuple-element.121, bf16[12,256,256]{2,1,0:T(8,128)(2,1)S(1)} %gather_fusion, bf16[12,256,256]{2,1,0:T(8,128)(2,1)S(1)} %get-tuple-element.120), kind=kOutput, calls=%fused_computation.6.clone.1 | convolution fusion | flops 806092800 | bytes 4980740 | tf_op jit(solution)/shard_map/while/body/eval_jaxpr/yxz,ysz->xs/dot_general | solution.py:28
  172.2 5.2 %gather_fusion = bf16[12,256,256]{2,1,0:T(8,128)(2,1)S(1)} fusion(bf16[96,256,256]{2,1,0:T(8,128)(2,1)} %get-tuple-element.119, s32[1024]{0:T(1024)S(1)} %pad_clamp_fusion.3), kind=kCustom, calls=%fused_computation.clone.1 | custom fusion | bytes 3145776 | tf_op jit(solution)/shard_map/while/body/eval_jaxpr/gather | solution.py:24
  177.4 3.5 %fusion.27 = f32[6,256,256]{2,1,0:T(8,128)} fusion(f32[6,256,256]{2,1,0:T(8,128)} %get-tuple-element.110, s32[]{:T(128)S(6)} %copy.38, bf16[12,256,256]{2,1,0:T(8,128)(2,1)} %get-tuple-element.121, bf16[12,256,256]{2,1,0:T(8,128)(2,1)S(1)} %gather_fusion, bf16[12,256,256]{2,1,0:T(8,128)(2,1)S(1)} %get-tuple-element.120), kind=kOutput, calls=%fused_computation.6.clone.1 | convolution fusion | flops 806092800 | bytes 4980740 | tf_op jit(solution)/shard_map/while/body/eval_jaxpr/yxz,ysz->xs/dot_general | solution.py:28
  180.9 5.2 %gather_fusion = bf16[12,256,256]{2,1,0:T(8,128)(2,1)S(1)} fusion(bf16[96,256,256]{2,1,0:T(8,128)(2,1)} %get-tuple-element.119, s32[1024]{0:T(1024)S(1)} %pad_clamp_fusion.3), kind=kCustom, calls=%fused_computation.clone.1 | custom fusion | bytes 3145776 | tf_op jit(solution)/shard_map/while/body/eval_jaxpr/gather | solution.py:24
  186.1 3.4 %fusion.27 = f32[6,256,256]{2,1,0:T(8,128)} fusion(f32[6,256,256]{2,1,0:T(8,128)} %get-tuple-element.110, s32[]{:T(128)S(6)} %copy.38, bf16[12,256,256]{2,1,0:T(8,128)(2,1)} %get-tuple-element.121, bf16[12,256,256]{2,1,0:T(8,128)(2,1)S(1)} %gather_fusion, bf16[12,256,256]{2,1,0:T(8,128)(2,1)S(1)} %get-tuple-element.120), kind=kOutput, calls=%fused_computation.6.clone.1 | convolution fusion | flops 806092800 | bytes 4980740 | tf_op jit(solution)/shard_map/while/body/eval_jaxpr/yxz,ysz->xs/dot_general | solution.py:28
  189.6 5.2 %gather_fusion = bf16[12,256,256]{2,1,0:T(8,128)(2,1)S(1)} fusion(bf16[96,256,256]{2,1,0:T(8,128)(2,1)} %get-tuple-element.119, s32[1024]{0:T(1024)S(1)} %pad_clamp_fusion.3), kind=kCustom, calls=%fused_computation.clone.1 | custom fusion | bytes 3145776 | tf_op jit(solution)/shard_map/while/body/eval_jaxpr/gather | solution.py:24
  194.8 3.4 %fusion.27 = f32[6,256,256]{2,1,0:T(8,128)} fusion(f32[6,256,256]{2,1,0:T(8,128)} %get-tuple-element.110, s32[]{:T(128)S(6)} %copy.38, bf16[12,256,256]{2,1,0:T(8,128)(2,1)} %get-tuple-element.121, bf16[12,256,256]{2,1,0:T(8,128)(2,1)S(1)} %gather_fusion, bf16[12,256,256]{2,1,0:T(8,128)(2,1)S(1)} %get-tuple-element.120), kind=kOutput, calls=%fused_computation.6.clone.1 | convolution fusion | flops 806092800 | bytes 4980740 | tf_op jit(solution)/shard_map/while/body/eval_jaxpr/yxz,ysz->xs/dot_general | solution.py:28
  198.3 5.2 %gather_fusion = bf16[12,256,256]{2,1,0:T(8,128)(2,1)S(1)} fusion(bf16[96,256,256]{2,1,0:T(8,128)(2,1)} %get-tuple-element.119, s32[1024]{0:T(1024)S(1)} %pad_clamp_fusion.3), kind=kCustom, calls=%fused_computation.clone.1 | custom fusion | bytes 3145776 | tf_op jit(solution)/shard_map/while/body/eval_jaxpr/gather | solution.py:24
  203.5 3.4 %fusion.27 = f32[6,256,256]{2,1,0:T(8,128)} fusion(f32[6,256,256]{2,1,0:T(8,128)} %get-tuple-element.110, s32[]{:T(128)S(6)} %copy.38, bf16[12,256,256]{2,1,0:T(8,128)(2,1)} %get-tuple-element.121, bf16[12,256,256]{2,1,0:T(8,128)(2,1)S(1)} %gather_fusion, bf16[12,256,256]{2,1,0:T(8,128)(2,1)S(1)} %get-tuple-element.120), kind=kOutput, calls=%fused_computation.6.clone.1 | convolution fusion | flops 806092800 | bytes 4980740 | tf_op jit(solution)/shard_map/while/body/eval_jaxpr/yxz,ysz->xs/dot_general | solution.py:28
  206.9 5.2 %gather_fusion = bf16[12,256,256]{2,1,0:T(8,128)(2,1)S(1)} fusion(bf16[96,256,256]{2,1,0:T(8,128)(2,1)} %get-tuple-element.119, s32[1024]{0:T(1024)S(1)} %pad_clamp_fusion.3), kind=kCustom, calls=%fused_computation.clone.1 | custom fusion | bytes 3145776 | tf_op jit(solution)/shard_map/while/body/eval_jaxpr/gather | solution.py:24
  212.2 3.4 %fusion.27 = f32[6,256,256]{2,1,0:T(8,128)} fusion(f32[6,256,256]{2,1,0:T(8,128)} %get-tuple-element.110, s32[]{:T(128)S(6)} %copy.38, bf16[12,256,256]{2,1,0:T(8,128)(2,1)} %get-tuple-element.121, bf16[12,256,256]{2,1,0:T(8,128)(2,1)S(1)} %gather_fusion, bf16[12,256,256]{2,1,0:T(8,128)(2,1)S(1)} %get-tuple-element.120), kind=kOutput, calls=%fused_computation.6.clone.1 | convolution fusion | flops 806092800 | bytes 4980740 | tf_op jit(solution)/shard_map/while/body/eval_jaxpr/yxz,ysz->xs/dot_general | solution.py:28
  215.6 0.7 dynamic-slice_bitcast_fusion
  216.4 0.3 convolution_bitcast_fusion
  216.6 103.1 %psum.7 = f32[4]{0:T(128)S(1)} all-reduce(f32[4]{0:T(128)S(1)} %convolution_bitcast_fusion), channel_id=1, replica_groups=mesh['term'=32,'sector'=16] {'term','sector'}, use_global_device_ids=true, to_apply=%region_3.4 | all-reduce | flops 4 | bytes 32 | tf_op jit(solution)/shard_map/psum | solution.py:44
  319.8 0.2 fusion.9
  320.0 1.4 bitcast_add_fusion
  (33 shorter events, 0.5 us)
Async XLA Ops:
  7.2 209.2 %copy-start = (bf16[4,6,8,256]{3,2,1,0:T(8,128)(2,1)S(1)}, bf16[4,6,8,256]{3,2,1,0:T(8,128)(2,1)}, u32[]{:S(2)}) copy-start(bf16[4,6,8,256]{3,2,1,0:T(8,128)(2,1)} %param.14) | copy-start | bytes 294916
  7.2 2.5 copy-start.1
  7.2 156.3 %all-gather.2.cloned.1.call-start = ((), (), s32[]{:S(2)}) async-start(), calls=%async_computation.1 | async-start | bytes 13369344 | tf_op jit(solution)/shard_map/all_gather | solution.py:20
  7.9 312.1 %reduce-scatter.2.cloned.1.call-start = ((), (), s32[]{:S(2)}) async-start(), calls=%async_computation.2 | async-start | bytes 1622016 | tf_op jit(solution)/shard_map/reduce_scatter | solution.py:36
  9.7 153.9 %copy-start.2 = (bf16[12,256,256]{2,1,0:T(8,128)(2,1)S(1)}, bf16[12,256,256]{2,1,0:T(8,128)(2,1)}, u32[]{:S(2)}) copy-start(bf16[12,256,256]{2,1,0:T(8,128)(2,1)} %param.10) | copy-start | bytes 4718596
  215.6 104.2 %copy-start.3 = (f32[4]{0:T(128)S(1)}, f32[4]{0:T(128)}, u32[]{:S(2)}) copy-start(f32[4]{0:T(128)} %param.15) | copy-start | bytes 52
  319.8 1.6 copy-start.4
Sparse Core Ops, SparseCore 0:
  10.1 153.3 all-gather.1
  215.8 97.6 reduce-scatter.1
where the time goes:
time: 329 us; the launch traced here: 328 us
  waiting for transfers between devices  153 us (47%)
  blocking collectives  103 us (31%)
  local copies, waits for them, and re-layouts  34.5 us (10%)
  matrix products  21 us (6%)
  between operations  14.1 us (4%)
    all_gather x1, waiting for transfers between devices, per_device(): store = lax.all_gather(wavefunction, 'sector', axis=0, tiled=True)  152 us
    psum x1, blocking collectives, per_device(): correlations = lax.psum(local_correlation, ('term', 'sector')) / total_cells  103 us
    gather x6, local copies, waits for them, and re-layouts, one_sector(): input_sectors = store[column]  31.3 us
    dot_general x6, matrix products, one_sector(): jnp.einsum('yxz,ysz->xs', partial_contraction, right_operator_blocks, pre...  20.6 us
  transfers between devices with their start and end apart: 2, of which 1 were waited for; matrix products, arithmetic and copies ran while one was open for 1% of the time, Pallas kernels for 0%

commit v1 on v0

--- a/solution.py
+++ b/solution.py
@@ -41,7 +41,7 @@
         "ksab,sab->k", lower_roots, psi_rows, preferred_element_type=jnp.float32
     )
     total_cells = lax.axis_size("sector") * sec_dev * block_width * block_width
-    correlations = lax.psum(local_correlation, ("term", "sector")) / total_cells
+    correlations = jnp.sum(lax.all_gather(local_correlation, ("term", "sector")), 0) / total_cells
     sigma = reduced + jnp.einsum(
         "k,ksab->sab", level_shift * correlations, lower_roots.astype(jnp.float32)
     )

time: 329 us -> 330 us (level)
    unnamed x0 -> x1, blocking collectives: none -> 103 us
    psum x1 -> x0, blocking collectives: 103 us -> none  [per_device(): correlations = lax.psum(local_correlation, ('term', 'sector')) / total_cells]
where the time goes in v1:
time: 330 us; the launch traced here: 329 us
  waiting for transfers between devices  153 us (46%)
  blocking collectives  103 us (31%)
  local copies, waits for them, and re-layouts  34.9 us (11%)
  matrix products  21 us (6%)
  between operations  14.1 us (4%)
    all_gather x1, waiting for transfers between devices, per_device(): store = lax.all_gather(wavefunction, 'sector', axis=0, tiled=True)  152 us
    unnamed x1, blocking collectives  103 us
    gather x6, local copies, waits for them, and re-layouts, one_sector(): input_sectors = store[column]  31.3 us
    dot_general x6, matrix products, one_sector(): jnp.einsum('yxz,ysz->xs', partial_contraction, right_operator_blocks, pre...  20.6 us
  transfers between devices with their start and end apart: 2, of which 1 were waited for; matrix products, arithmetic and copies ran while one was open for 1% of the time, Pallas kernels for 0%

profile of v1, /device:TPU:1, one launch (start us, length us, event | category | flops | bytes accessed | tf_op | source)
XLA Modules:
  0.0 328.9 jit_solution(9994035775407411090)
XLA Ops:
  7.2 0.7 all-gather.3.cloned.1.call-update
  8.0 0.8 copy.17
  8.8 0.7 compare_select_fusion.1
  9.7 1.2 gather_fusion.1
  11.1 152.4 %all-gather.3.cloned.1.call-done = bf16[96,256,256]{2,1,0:T(8,128)(2,1)} async-done(((bf16[6,256,256]{2,1,0:T(8,128)(2,1)}), bf16[96,256,256]{2,1,0:T(8,128)(2,1)}) %all-gather.3.cloned.1.call-update) | async-done | bytes 12582928 | tf_op jit(solution)/shard_map/all_gather | solution.py:20
  163.5 52.1 %while.10 = (s32[]{:T(128)}, f32[6,256,256]{2,1,0:T(8,128)}, s32[6,12]{1,0:T(8,128)S(1)}, bf16[96,256,256]{2,1,0:T(8,128)(2,1)}, bf16[12,256,256]{2,1,0:T(8,128)...) while((s32[]{:T(128)}, f32[6,256,256]{2,1,0:T(8,128)}, s32[6,12]{1,0:T(8,128)S(1)}, ...), condition=%wide.region_1.2_spmd, body=%wide.region_0.1_spmd.sunk | while | flops 806093888 | bytes 8130845 | solution.py:35
  163.5 5.2 %gather_fusion = bf16[12,256,256]{2,1,0:T(8,128)(2,1)S(1)} fusion(bf16[96,256,256]{2,1,0:T(8,128)(2,1)} %get-tuple-element.119, s32[1024]{0:T(1024)S(1)} %pad_clamp_fusion.3), kind=kCustom, calls=%fused_computation.clone.1 | custom fusion | bytes 3145776 | tf_op jit(solution)/shard_map/while/body/eval_jaxpr/gather | solution.py:24
  168.8 3.4 %fusion.27 = f32[6,256,256]{2,1,0:T(8,128)} fusion(f32[6,256,256]{2,1,0:T(8,128)} %get-tuple-element.110, s32[]{:T(128)S(6)} %copy.38, bf16[12,256,256]{2,1,0:T(8,128)(2,1)} %get-tuple-element.121, bf16[12,256,256]{2,1,0:T(8,128)(2,1)S(1)} %gather_fusion, bf16[12,256,256]{2,1,0:T(8,128)(2,1)S(1)} %get-tuple-element.120), kind=kOutput, calls=%fused_computation.6.clone.1 | convolution fusion | flops 806092800 | bytes 4980740 | tf_op jit(solution)/shard_map/while/body/eval_jaxpr/yxz,ysz->xs/dot_general | solution.py:28
  172.2 5.2 %gather_fusion = bf16[12,256,256]{2,1,0:T(8,128)(2,1)S(1)} fusion(bf16[96,256,256]{2,1,0:T(8,128)(2,1)} %get-tuple-element.119, s32[1024]{0:T(1024)S(1)} %pad_clamp_fusion.3), kind=kCustom, calls=%fused_computation.clone.1 | custom fusion | bytes 3145776 | tf_op jit(solution)/shard_map/while/body/eval_jaxpr/gather | solution.py:24
  177.4 3.4 %fusion.27 = f32[6,256,256]{2,1,0:T(8,128)} fusion(f32[6,256,256]{2,1,0:T(8,128)} %get-tuple-element.110, s32[]{:T(128)S(6)} %copy.38, bf16[12,256,256]{2,1,0:T(8,128)(2,1)} %get-tuple-element.121, bf16[12,256,256]{2,1,0:T(8,128)(2,1)S(1)} %gather_fusion, bf16[12,256,256]{2,1,0:T(8,128)(2,1)S(1)} %get-tuple-element.120), kind=kOutput, calls=%fused_computation.6.clone.1 | convolution fusion | flops 806092800 | bytes 4980740 | tf_op jit(solution)/shard_map/while/body/eval_jaxpr/yxz,ysz->xs/dot_general | solution.py:28
  180.9 5.2 %gather_fusion = bf16[12,256,256]{2,1,0:T(8,128)(2,1)S(1)} fusion(bf16[96,256,256]{2,1,0:T(8,128)(2,1)} %get-tuple-element.119, s32[1024]{0:T(1024)S(1)} %pad_clamp_fusion.3), kind=kCustom, calls=%fused_computation.clone.1 | custom fusion | bytes 3145776 | tf_op jit(solution)/shard_map/while/body/eval_jaxpr/gather | solution.py:24
  186.1 3.4 %fusion.27 = f32[6,256,256]{2,1,0:T(8,128)} fusion(f32[6,256,256]{2,1,0:T(8,128)} %get-tuple-element.110, s32[]{:T(128)S(6)} %copy.38, bf16[12,256,256]{2,1,0:T(8,128)(2,1)} %get-tuple-element.121, bf16[12,256,256]{2,1,0:T(8,128)(2,1)S(1)} %gather_fusion, bf16[12,256,256]{2,1,0:T(8,128)(2,1)S(1)} %get-tuple-element.120), kind=kOutput, calls=%fused_computation.6.clone.1 | convolution fusion | flops 806092800 | bytes 4980740 | tf_op jit(solution)/shard_map/while/body/eval_jaxpr/yxz,ysz->xs/dot_general | solution.py:28
  189.6 5.2 %gather_fusion = bf16[12,256,256]{2,1,0:T(8,128)(2,1)S(1)} fusion(bf16[96,256,256]{2,1,0:T(8,128)(2,1)} %get-tuple-element.119, s32[1024]{0:T(1024)S(1)} %pad_clamp_fusion.3), kind=kCustom, calls=%fused_computation.clone.1 | custom fusion | bytes 3145776 | tf_op jit(solution)/shard_map/while/body/eval_jaxpr/gather | solution.py:24
  194.8 3.4 %fusion.27 = f32[6,256,256]{2,1,0:T(8,128)} fusion(f32[6,256,256]{2,1,0:T(8,128)} %get-tuple-element.110, s32[]{:T(128)S(6)} %copy.38, bf16[12,256,256]{2,1,0:T(8,128)(2,1)} %get-tuple-element.121, bf16[12,256,256]{2,1,0:T(8,128)(2,1)S(1)} %gather_fusion, bf16[12,256,256]{2,1,0:T(8,128)(2,1)S(1)} %get-tuple-element.120), kind=kOutput, calls=%fused_computation.6.clone.1 | convolution fusion | flops 806092800 | bytes 4980740 | tf_op jit(solution)/shard_map/while/body/eval_jaxpr/yxz,ysz->xs/dot_general | solution.py:28
  198.3 5.2 %gather_fusion = bf16[12,256,256]{2,1,0:T(8,128)(2,1)S(1)} fusion(bf16[96,256,256]{2,1,0:T(8,128)(2,1)} %get-tuple-element.119, s32[1024]{0:T(1024)S(1)} %pad_clamp_fusion.3), kind=kCustom, calls=%fused_computation.clone.1 | custom fusion | bytes 3145776 | tf_op jit(solution)/shard_map/while/body/eval_jaxpr/gather | solution.py:24
  203.5 3.4 %fusion.27 = f32[6,256,256]{2,1,0:T(8,128)} fusion(f32[6,256,256]{2,1,0:T(8,128)} %get-tuple-element.110, s32[]{:T(128)S(6)} %copy.38, bf16[12,256,256]{2,1,0:T(8,128)(2,1)} %get-tuple-element.121, bf16[12,256,256]{2,1,0:T(8,128)(2,1)S(1)} %gather_fusion, bf16[12,256,256]{2,1,0:T(8,128)(2,1)S(1)} %get-tuple-element.120), kind=kOutput, calls=%fused_computation.6.clone.1 | convolution fusion | flops 806092800 | bytes 4980740 | tf_op jit(solution)/shard_map/while/body/eval_jaxpr/yxz,ysz->xs/dot_general | solution.py:28
  206.9 5.2 %gather_fusion = bf16[12,256,256]{2,1,0:T(8,128)(2,1)S(1)} fusion(bf16[96,256,256]{2,1,0:T(8,128)(2,1)} %get-tuple-element.119, s32[1024]{0:T(1024)S(1)} %pad_clamp_fusion.3), kind=kCustom, calls=%fused_computation.clone.1 | custom fusion | bytes 3145776 | tf_op jit(solution)/shard_map/while/body/eval_jaxpr/gather | solution.py:24
  212.2 3.4 %fusion.27 = f32[6,256,256]{2,1,0:T(8,128)} fusion(f32[6,256,256]{2,1,0:T(8,128)} %get-tuple-element.110, s32[]{:T(128)S(6)} %copy.38, bf16[12,256,256]{2,1,0:T(8,128)(2,1)} %get-tuple-element.121, bf16[12,256,256]{2,1,0:T(8,128)(2,1)S(1)} %gather_fusion, bf16[12,256,256]{2,1,0:T(8,128)(2,1)S(1)} %get-tuple-element.120), kind=kOutput, calls=%fused_computation.6.clone.1 | convolution fusion | flops 806092800 | bytes 4980740 | tf_op jit(solution)/shard_map/while/body/eval_jaxpr/yxz,ysz->xs/dot_general | solution.py:28
  215.6 0.7 dynamic-slice_bitcast_fusion
  216.4 0.3 convolution_bitcast_fusion
  216.6 0.2 dynamic-update-slice
  216.8 103.2 %all-reduce = f32[2048]{0:T(1024)S(1)} all-reduce(f32[2048]{0:T(1024)S(1)} %dynamic-update-slice), channel_id=2, replica_groups=mesh['term'=32,'sector'=16] {'term','sector'}, use_global_device_ids=true, to_apply=%add | all-reduce | flops 2048 | bytes 16384
  320.0 0.3 reshape.48
  320.6 1.4 bitcast_add_fusion
  (37 shorter events, 0.9 us)
Async XLA Ops:
  7.2 209.2 %copy-start = (bf16[4,6,8,256]{3,2,1,0:T(8,128)(2,1)S(1)}, bf16[4,6,8,256]{3,2,1,0:T(8,128)(2,1)}, u32[]{:S(2)}) copy-start(bf16[4,6,8,256]{3,2,1,0:T(8,128)(2,1)} %param.14) | copy-start | bytes 294916
  7.2 2.5 copy-start.1
  7.2 156.3 %all-gather.3.cloned.1.call-start = ((), (), s32[]{:S(2)}) async-start(), calls=%async_computation.1 | async-start | bytes 13369344 | tf_op jit(solution)/shard_map/all_gather | solution.py:20
  7.9 312.7 %reduce-scatter.2.cloned.1.call-start = ((), (), s32[]{:S(2)}) async-start(), calls=%async_computation.2 | async-start | bytes 1622016 | tf_op jit(solution)/shard_map/reduce_scatter | solution.py:36
  9.7 153.9 %copy-start.2 = (bf16[12,256,256]{2,1,0:T(8,128)(2,1)S(1)}, bf16[12,256,256]{2,1,0:T(8,128)(2,1)}, u32[]{:S(2)}) copy-start(bf16[12,256,256]{2,1,0:T(8,128)(2,1)} %param.10) | copy-start | bytes 4718596
  215.6 104.8 %copy-start.3 = (f32[4]{0:T(128)S(1)}, f32[4]{0:T(128)}, u32[]{:S(2)}) copy-start(f32[4]{0:T(128)} %param.15) | copy-start | bytes 52
  320.4 1.7 copy-start.4
Sparse Core Ops, SparseCore 0:
  10.1 153.3 all-gather.2
  215.7 97.5 reduce-scatter.1
